TPU v7x, 32 devices: a whole 2x2x4 slice. The times are simulated.
32 devices in a mesh: pole: 2 (over y), prow: 1, pcol: 16 (over z, x, core).
Axes of the slice: x: 2, y: 2, z: 4, core: 2. Of those that a mesh axis runs over, the one named last changes fastest.
Arguments:
- anc_inverse: float32 [12288, 6144], P(('pole', 'prow'), 'pcol'), parts along dimension 0, may hold values from -8 to 8
- anc_factor: float32 [12288, 768], P(('pole', 'pcol')), parts along dimension 0, may hold values from -0.078125 to 0.078125
- win_factor: float32 [1536, 768], P('pole'), parts along dimension 0, may hold values from -0.375 to 0.375
- pivot_inverse: float32 [6, 256, 256], P('pole'), parts along dimension 0, may hold values from -6 to 6
- structure: int32 [3, 24], replicated, may hold values 0 or 1
Outputs:
- anc_columns: float32 [12288, 768], P(('pole', 'prow', 'pcol')), parts along dimension 0
- win_inverse: float32 [1536, 768], P('pole'), parts along dimension 0
There are 2 independent parts, one for each index of `pole`. A program takes and returns all parts, laid end to end along the dimension named above; an argument that names none is the same for every part. Nothing has to cross between parts.
All inputs are finite; a program needn't handle non-finite values.
Results may differ from a plain program's by a relative error of at most 0.0001.
Values sent between devices are 32-bit elements; how exact they have to be, the bound alone decides.
A program may use at most 128 MiB of HBM per device.

v0:
```python
import jax
import jax.numpy as jnp
from jax import lax
from jax.sharding import PartitionSpec as P

precise = lax.Precision.HIGHEST


def product(left, right):
    return jnp.dot(left, right, precision=precise, preferred_element_type=jnp.float32)


def on_device(anc_inverse, anc_factor, win_factor, pivot_inverse, structure):
    row_count = lax.axis_size("prow")
    col_count = lax.axis_size("pcol")
    row_index = lax.axis_index("prow")
    col_index = lax.axis_index("pcol")
    block_rows = anc_inverse.shape[0]
    block_cols = anc_inverse.shape[1]
    steps_total = pivot_inverse.shape[0]
    width = pivot_inverse.shape[1]
    all_cols = anc_factor.shape[1]
    block_count = structure.shape[1]
    ratio_cols = col_count // row_count
    share_rows = block_rows // col_count
    structure_cols = structure.T.astype(jnp.float32)
    global_rows = col_index * block_cols + lax.iota(jnp.int32, block_cols)
    onehot_rows = (
        (global_rows // width)[:, None] == lax.iota(jnp.int32, block_count)[None, :]
    ).astype(jnp.float32)
    kept_rows = product(onehot_rows, structure_cols)
    share_offset = col_index * share_rows
    share_global = (row_index * col_count + col_index) * share_rows + lax.iota(
        jnp.int32, share_rows
    )
    onehot_share = (
        (share_global // width)[:, None] == lax.iota(jnp.int32, block_count)[None, :]
    ).astype(jnp.float32)
    kept_share = product(onehot_share, structure_cols)
    slot_ids = lax.iota(jnp.int32, col_count)
    source_flag = (slot_ids // row_count == col_index - row_index * ratio_cols).astype(jnp.float32)
    pieces = jnp.tile(anc_factor.reshape(row_count, share_rows, all_cols), (ratio_cols, 1, 1))
    outgoing = pieces * source_flag[:, None, None]
    incoming = lax.all_to_all(outgoing, "pcol", split_axis=0, concat_axis=0, tiled=True)
    factor_share = jnp.sum(incoming, axis=0)
    column_store = {}
    share_store = {}
    window_blocks = {}
    for k in range(steps_total - 1, -1, -1):
        first_col = k * width
        factor_now = anc_factor[:, first_col : first_col + width] * kept_rows[:, k : k + 1]
        share_factor = factor_share[:, first_col : first_col + width] * kept_share[:, k : k + 1]
        finished = list(range(k + 1, steps_total))
        if finished:
            stacked = jnp.concatenate([column_store[j] for j in finished], axis=1)
            factor_win = win_factor[first_col + width :, first_col : first_col + width]

        def term_rows(start, count, factor_now=factor_now):
            return product(anc_inverse, factor_now)

        share_image = lax.psum_scatter(
            term_rows(jnp.int32(0), share_rows * lax.axis_size("pcol")),
            "pcol",
            scatter_dimension=0,
            tiled=True,
        )
        if finished:
            share_image = share_image + product(
                lax.dynamic_slice_in_dim(stacked, share_offset, share_rows, 0), factor_win
            )
        share_column = -share_image
        column_now = lax.all_gather(share_column, "pcol", axis=0, tiled=True)
        crossings = [product(share_store[j].T, share_factor) for j in finished]
        pivot_part = product(share_factor.T, share_column)
        cross_sums = []
        if finished:
            cross_total = lax.psum(jnp.stack(crossings), ("prow", "pcol"))
            cross_sums = [cross_total[position] for position in range(len(finished))]
        pivot_sum = lax.psum(pivot_part, ("prow", "pcol"))
        for position, j in enumerate(finished):
            running = cross_sums[position]
            for i in finished:
                running = running + product(
                    window_blocks[j, i],
                    win_factor[i * width : (i + 1) * width, first_col : first_col + width],
                )
            window_blocks[j, k] = -running
            window_blocks[k, j] = -running.T
        pivot_block = pivot_inverse[k] - pivot_sum
        for j in finished:
            pivot_block = pivot_block - product(
                win_factor[j * width : (j + 1) * width, first_col : first_col + width].T,
                window_blocks[j, k],
            )
        window_blocks[k, k] = pivot_block
        column_store[k] = column_now
        share_store[k] = share_column
    anc_columns = jnp.concatenate([share_store[k] for k in range(steps_total)], axis=1)
    win_inverse = jnp.concatenate(
        [
            jnp.concatenate([window_blocks[i, k] for k in range(steps_total)], axis=1)
            for i in range(steps_total)
        ],
        axis=0,
    )
    return (anc_columns, win_inverse)


def solution(mesh):
    in_specs = (
        P(("pole", "prow"), "pcol"),
        P(("pole", "pcol"), None),
        P("pole", None),
        P("pole", None, None),
        P(),
    )
    out_specs = (P(("pole", "prow", "pcol"), None), P("pole", None))
    return jax.shard_map(
        on_device, mesh=mesh, in_specs=in_specs, out_specs=out_specs, check_vma=False
    )
```

profile of v0, /device:TPU:0, one launch (start us, length us, event | category | flops | bytes accessed | tf_op | source)
XLA Modules:
  0.0 905.3 jit_solution(14524148858973868540)
XLA Ops:
  7.2 0.0 reduce-scatter.8.cloned.1.call-start
  7.2 1.0 fusion.40
  8.2 19.4 %convolution_bitcast_fusion = f32[6144,256]{0,1:T(8,128)} fusion(f32[6144,384]{1,0:T(8,128)} %param.5, f32[384,768]{1,0:T(8,128)} %param.6, f32[384]{0:T(512)S(1)} %get-tuple-element.7), kind=kOutput, calls=%fused_computation.3 | convolution fusion | flops 7247855616 | bytes 16123392 | tf_op jit(solution)/shard_map/dot_general | solution.py:10
  27.6 0.0 reduce-scatter.8.cloned.1.call-update
  27.6 0.2 reduce-scatter.6.cloned.1.call-start
  27.9 1.0 copy-done.2
  28.9 19.2 %convolution_bitcast_fusion.1 = f32[6144,256]{0,1:T(8,128)} fusion(f32[6144,384]{1,0:T(8,128)} %param.5, f32[384,768]{1,0:T(8,128)S(1)} %copy-done.2, f32[384]{0:T(512)S(1)} %get-tuple-element.8), kind=kOutput, calls=%fused_computation.4 | convolution fusion | flops 7247855616 | bytes 16123904 | tf_op jit(solution)/shard_map/dot_general | solution.py:10
  48.1 0.0 reduce-scatter.6.cloned.1.call-update
  48.1 8.4 broadcast_multiply_fusion
  56.5 7.4 all-to-all-start
  63.9 0.0 all-gather.3.cloned.1.call-start
  63.9 346.9 %reduce-scatter.8.cloned.1.call-done = f32[384,256]{0,1:T(8,128)} async-done(((f32[6144,256]{0,1:T(8,128)}), f32[384,256]{0,1:T(8,128)}) %reduce-scatter.8.cloned.1.call-update) | async-done | bytes 393232 | tf_op jit(solution)/shard_map/reduce_scatter | solution.py:61
  410.8 1.8 neg.30
  412.6 0.0 all-gather.3.cloned.1.call-update
  412.6 0.3 reduce-scatter.4.cloned.1.call-start
  412.9 19.2 %convolution_bitcast_fusion.2 = f32[6144,256]{0,1:T(8,128)} fusion(f32[6144,384]{1,0:T(8,128)} %param.5, f32[384,768]{1,0:T(8,128)S(1)} %copy-done.2, f32[384]{0:T(512)S(1)} %get-tuple-element.6), kind=kOutput, calls=%fused_computation.5 | convolution fusion | flops 7247855616 | bytes 16123904 | tf_op jit(solution)/shard_map/dot_general | solution.py:10
  432.1 0.0 reduce-scatter.4.cloned.1.call-update
  432.1 0.0 all-gather.5.cloned.1.call-start
  432.2 121.9 %reduce-scatter.6.cloned.1.call-done = f32[384,256]{0,1:T(8,128)} async-done(((f32[6144,256]{0,1:T(8,128)}), f32[384,256]{0,1:T(8,128)}) %reduce-scatter.6.cloned.1.call-update) | async-done | bytes 393232 | tf_op jit(solution)/shard_map/reduce_scatter | solution.py:61
  554.1 64.0 %all-gather.3.cloned.1.call-done = f32[6144,256]{0,1:T(8,128)} async-done(((f32[384,256]{0,1:T(8,128)}), f32[6144,256]{0,1:T(8,128)}) %all-gather.3.cloned.1.call-update) | async-done | bytes 6291472 | tf_op jit(solution)/shard_map/all_gather | solution.py:72
  618.1 2.6 fusion.1
  620.7 0.0 all-gather.5.cloned.1.call-update
  620.7 0.3 all-reduce.3.cloned.1.call-start
  621.0 84.6 %reduce-scatter.4.cloned.1.call-done = f32[384,256]{0,1:T(8,128)} async-done(((f32[6144,256]{0,1:T(8,128)}), f32[384,256]{0,1:T(8,128)}) %reduce-scatter.4.cloned.1.call-update) | async-done | bytes 393232 | tf_op jit(solution)/shard_map/reduce_scatter | solution.py:61
  705.7 64.0 %all-gather.5.cloned.1.call-done = f32[6144,256]{0,1:T(8,128)} async-done(((f32[384,256]{0,1:T(8,128)}), f32[6144,256]{0,1:T(8,128)}) %all-gather.5.cloned.1.call-update) | async-done | bytes 6291472 | tf_op jit(solution)/shard_map/all_gather | solution.py:72
  769.7 2.4 fusion
  772.1 0.0 copy-start
  772.1 0.0 all-to-all-done
  772.1 7.7 reduce_sum.9
  779.8 0.0 copy-done
  779.8 0.0 copy-start.1
  779.8 0.9 convolution_bitcast_fusion.7
  780.7 1.4 fusion.20
  782.1 1.6 fusion.21
  783.7 0.0 copy-done.1
  783.7 0.9 convolution_bitcast_fusion.6
  784.6 0.8 pad_maximum_fusion.2
  785.4 1.4 fusion.19
  786.8 1.6 fusion.11
  788.3 0.0 all-reduce.3.cloned.1.call-update
  788.4 0.0 slice-done
  788.4 0.8 copy.42
  789.2 0.0 copy-done.3
  789.2 0.1 pad_maximum_fusion
  789.3 1.4 copy.32
  790.7 93.1 %all-reduce.3.cloned.1.call-done = (f32[256,256]{1,0:T(8,128)}, f32[256,256]{1,0:T(8,128)}, f32[2,256,256]{1,2,0:T(8,128)}, f32[256,256]{0,1:T(8,128)}, f32[256,256]{1,0:T(8,128)}) async-done(((f32[256,256]{1,0:T(8,128)}, f32[256,256]{1,0:T(8,128)}, f32[2,256,256]{1,2,0:T(8,128)}, f32[256,256]{0,1:T(8,128)}, f32[256,256]{1,0:T(8,128)}), (f32[256,256]{1,0:T(8,128)}, f32[256,256]{1,0:T(8,128)}, ...) | async-done | bytes 1572880 | tf_op jit(solution)/shard_map/psum | solution.py:79
  883.8 1.1 bitcast_subtract_fusion
  884.9 1.4 fusion.7
  886.3 1.6 convolution_add_fusion.3
  887.9 0.0 copy-done.4
  888.0 1.5 fusion.6
  889.5 0.7 copy-done.5
  890.2 0.0 copy-done.10
  890.2 0.6 convolution_add_fusion.5
  890.8 0.6 fusion.5
  891.4 0.6 fusion.3
  892.0 0.8 copy.30
  892.9 1.7 fusion.4
  894.6 1.3 fusion.2
  895.9 0.1 pad_maximum_fusion.1
  895.9 0.3 copy.31
  896.2 0.6 copy-done.8
  896.8 0.1 copy-done.9
  896.9 1.6 maximum_maximum_fusion
  (15 shorter events, 0.1 us)
Async XLA Ops:
  7.2 403.7 %reduce-scatter.8.cloned.1.call-start = ((), (), s32[]{:S(2)}) async-start(), calls=%async_computation.6 | async-start | bytes 6684672 | tf_op jit(solution)/shard_map/reduce_scatter | solution.py:61
  27.6 1.3 copy-start.2
  27.6 526.5 %reduce-scatter.6.cloned.1.call-start = ((), (), s32[]{:S(2)}) async-start(), calls=%async_computation.5 | async-start | bytes 6684672 | tf_op jit(solution)/shard_map/reduce_scatter | solution.py:61
  56.5 715.6 %all-to-all-start = ((f32[16,384,768]{2,1,0:T(8,128)}), f32[16,384,768]{2,1,0:T(8,128)}, u32[]{:S(2)}, u32[]{:S(2)}) async-start(f32[16,384,768]{2,1,0:T(8,128)} %broadcast_multiply_fusion), calls=%async_computation.3 | async-start | bytes 37748736 | tf_op jit(solution)/shard_map/all_to_all | solution.py:44
  63.9 554.3 %all-gather.3.cloned.1.call-start = ((), (), s32[]{:S(2)}) async-start(), calls=%async_computation.7 | async-start | bytes 6684672 | tf_op jit(solution)/shard_map/all_gather | solution.py:72
  412.6 293.1 %reduce-scatter.4.cloned.1.call-start = ((), (), s32[]{:S(2)}) async-start(), calls=%async_computation.4 | async-start | bytes 6684672 | tf_op jit(solution)/shard_map/reduce_scatter | solution.py:61
  432.1 337.5 %all-gather.5.cloned.1.call-start = ((), (), s32[]{:S(2)}) async-start(), calls=%async_computation.8 | async-start | bytes 6684672 | tf_op jit(solution)/shard_map/all_gather | solution.py:72
  620.7 263.0 %all-reduce.3.cloned.1.call-start = ((), (), s32[]{:S(2)}) async-start(), calls=%async_computation.9 | async-start | bytes 3145728 | tf_op jit(solution)/shard_map/psum | solution.py:79
  772.1 7.7 copy-start
  779.8 3.9 copy-start.1
  785.4 3.0 slice-start
  785.4 3.8 copy-start.3
  790.7 97.3 %copy-start.4 = (f32[768,768]{1,0:T(8,128)S(1)}, f32[768,768]{1,0:T(8,128)}, u32[]{:S(2)}) copy-start(f32[768,768]{1,0:T(8,128)} %param.7) | copy-start | bytes 7077892
  790.7 97.3 %copy-start.7 = (f32[1,256,256]{1,2,0:T(8,128)S(1)}, f32[1,256,256]{1,2,0:T(8,128)}, u32[]{:S(2)}) copy-start(f32[1,256,256]{1,2,0:T(8,128)} %copy.42) | copy-start | bytes 786436
  883.8 6.5 copy-start.10
  889.5 0.7 copy-start.5
  892.9 3.0 copy-start.6
  895.9 0.9 copy-start.8
  895.9 1.0 copy-start.9
Sparse Core Ops, SparseCore 0:
  27.8 383.0 reduce-scatter.7
  415.3 138.7 reduce-scatter.5
  557.0 61.1 all-gather.2
  621.9 83.6 reduce-scatter.3
  708.7 60.9 all-gather.4
  788.5 95.2 all-reduce.2
where the time goes:
time: 906 us; the launch traced here: 905 us
  waiting for transfers between devices  775 us (86%)
  matrix products  80.8 us (9%)
  other arithmetic  21.5 us (2%)
  between operations  14.3 us (2%)
    reduce_scatter x3, waiting for transfers between devices, on_device(): lax.psum_scatter(term_rows(jnp.int32(0), share_rows * lax.axis_size('pcol...  553 us
    all_gather x2, waiting for transfers between devices, on_device(): column_now = lax.all_gather(share_column, 'pcol', axis=0, tiled=True)  128 us
    psum x1, waiting for transfers between devices, on_device(): pivot_sum = lax.psum(pivot_part, ('prow', 'pcol'))  93.1 us
    dot_general x20, matrix products, product(): jnp.dot(left, right, precision=precise, preferred_element_type=jnp.float32)  80.8 us
  transfers between devices with their start and end apart: 7, of which 6 were waited for; matrix products, arithmetic and copies ran while one was open for 6% of the time, Pallas kernels for 0%

commit v1 on v0

--- a/solution.py
+++ b/solution.py
@@ -76,7 +76,8 @@
         if finished:
             cross_total = lax.psum(jnp.stack(crossings), ("prow", "pcol"))
             cross_sums = [cross_total[position] for position in range(len(finished))]
-        pivot_sum = lax.psum(pivot_part, ("prow", "pcol"))
+        parts = lax.all_gather(pivot_part, ("prow", "pcol"), axis=0, tiled=False)
+        pivot_sum = parts.sum(axis=0)
         for position, j in enumerate(finished):
             running = cross_sums[position]
             for i in finished:

time: 906 us -> 1040 us (1.15)
  waiting for transfers between devices: 775 us -> 894 us
    all_gather x0 -> x3, waiting for transfers between devices: none -> 137 us  [on_device(): parts = lax.all_gather(pivot_part, ('prow', 'pcol'), axis=0, tiled=False)]
    reduce_scatter x3, waiting for transfers between devices: 553 us -> 538 us  [on_device(): lax.psum_scatter(term_rows(jnp.int32(0), share_rows * lax.axis_size('pcol...]
  transfers between devices with their start and end apart: 7 -> 10, of which waited for: 6 -> 9; matrix products, arithmetic and copies ran while one was open for 6% -> 8% of each run, Pallas kernels for 0% -> 0%
where the time goes in v1:
time: 1040 us; the launch traced here: 1030 us
  waiting for transfers between devices  894 us (86%)
  matrix products  79.7 us (8%)
  other arithmetic  30.6 us (3%)
  between operations  14.1 us (1%)
    reduce_scatter x3, waiting for transfers between devices, on_device(): lax.psum_scatter(term_rows(jnp.int32(0), share_rows * lax.axis_size('pcol...  538 us
    all_gather x3, waiting for transfers between devices, on_device(): parts = lax.all_gather(pivot_part, ('prow', 'pcol'), axis=0, tiled=False)  137 us
    all_gather x2, waiting for transfers between devices, on_device(): column_now = lax.all_gather(share_column, 'pcol', axis=0, tiled=True)  127 us
    psum x1, waiting for transfers between devices, on_device(): cross_total = lax.psum(jnp.stack(crossings), ('prow', 'pcol'))  91.6 us
    dot_general x20, matrix products, product(): jnp.dot(left, right, precision=precise, preferred_element_type=jnp.float32)  79.7 us
  transfers between devices with their start and end apart: 10, of which 9 were waited for; matrix products, arithmetic and copies ran while one was open for 8% of the time, Pallas kernels for 0%

profile of v1, /device:TPU:0, one launch (start us, length us, event | category | flops | bytes accessed | tf_op | source)
XLA Modules:
  0.0 1034.8 jit_solution(10793104647366736843)
XLA Ops:
  7.2 0.0 reduce-scatter.8.cloned.1.call-start
  7.2 1.0 fusion.40
  8.2 19.4 %convolution_bitcast_fusion = f32[6144,256]{0,1:T(8,128)} fusion(f32[6144,384]{1,0:T(8,128)} %param.5, f32[384,768]{1,0:T(8,128)} %param.6, f32[384]{0:T(512)S(1)} %get-tuple-element.9), kind=kOutput, calls=%fused_computation.3 | convolution fusion | flops 7247855616 | bytes 16123392 | tf_op jit(solution)/shard_map/dot_general | solution.py:10
  27.6 0.0 reduce-scatter.8.cloned.1.call-update
  27.7 0.2 reduce-scatter.6.cloned.1.call-start
  27.9 1.0 copy-done.2
  28.9 19.3 %convolution_bitcast_fusion.1 = f32[6144,256]{0,1:T(8,128)} fusion(f32[6144,384]{1,0:T(8,128)} %param.5, f32[384,768]{1,0:T(8,128)S(1)} %copy-done.2, f32[384]{0:T(512)S(1)} %get-tuple-element.10), kind=kOutput, calls=%fused_computation.4 | convolution fusion | flops 7247855616 | bytes 16123904 | tf_op jit(solution)/shard_map/dot_general | solution.py:10
  48.2 8.4 broadcast_multiply_fusion
  56.6 7.4 all-to-all-start
  64.0 0.0 all-gather.9.cloned.1.call-start
  64.0 346.8 %reduce-scatter.8.cloned.1.call-done = f32[384,256]{0,1:T(8,128)} async-done(((f32[6144,256]{0,1:T(8,128)}), f32[384,256]{0,1:T(8,128)}) %reduce-scatter.8.cloned.1.call-update) | async-done | bytes 393232 | tf_op jit(solution)/shard_map/reduce_scatter | solution.py:61
  410.8 1.8 neg.30
  412.6 0.3 reduce-scatter.4.cloned.1.call-start
  412.9 19.3 %convolution_bitcast_fusion.2 = f32[6144,256]{0,1:T(8,128)} fusion(f32[6144,384]{1,0:T(8,128)} %param.5, f32[384,768]{1,0:T(8,128)S(1)} %copy-done.2, f32[384]{0:T(512)S(1)} %get-tuple-element.8), kind=kOutput, calls=%fused_computation.5 | convolution fusion | flops 7247855616 | bytes 16123904 | tf_op jit(solution)/shard_map/dot_general | solution.py:10
  432.1 0.0 reduce-scatter.4.cloned.1.call-update
  432.2 0.0 all-gather.11.cloned.1.call-start
  432.2 121.9 %reduce-scatter.6.cloned.1.call-done = f32[384,256]{0,1:T(8,128)} async-done(((f32[6144,256]{0,1:T(8,128)}), f32[384,256]{0,1:T(8,128)}) %reduce-scatter.6.cloned.1.call-update) | async-done | bytes 393232 | tf_op jit(solution)/shard_map/reduce_scatter | solution.py:61
  554.1 63.9 %all-gather.9.cloned.1.call-done = f32[6144,256]{0,1:T(8,128)} async-done(((f32[384,256]{0,1:T(8,128)}), f32[6144,256]{0,1:T(8,128)}) %all-gather.9.cloned.1.call-update) | async-done | bytes 6291472 | tf_op jit(solution)/shard_map/all_gather | solution.py:72
  618.0 2.6 fusion.1
  620.6 0.0 all-gather.11.cloned.1.call-update
  620.6 0.0 all-gather.17.cloned.1.call-start
  620.7 8.0 reduce_sum.36
  628.7 1.6 fusion.11
  630.3 0.0 all-gather.17.cloned.1.call-update
  630.3 0.0 all-reduce.3.cloned.1.call-start
  630.4 0.7 convolution_bitcast_fusion.7
  631.0 0.7 convolution_bitcast_fusion.6
  631.7 0.8 pad_maximum_fusion.2
  632.5 1.6 fusion.19
  634.1 0.0 all-reduce.3.cloned.1.call-update
  634.2 0.0 all-gather.15.cloned.1.call-start
  634.2 1.6 fusion.20
  635.8 0.3 all-gather.13.cloned.1.call-start
  636.1 69.4 %reduce-scatter.4.cloned.1.call-done = f32[384,256]{0,1:T(8,128)} async-done(((f32[6144,256]{0,1:T(8,128)}), f32[384,256]{0,1:T(8,128)}) %reduce-scatter.4.cloned.1.call-update) | async-done | bytes 393232 | tf_op jit(solution)/shard_map/reduce_scatter | solution.py:61
  705.5 63.4 %all-gather.11.cloned.1.call-done = f32[6144,256]{0,1:T(8,128)} async-done(((f32[384,256]{0,1:T(8,128)}), f32[6144,256]{0,1:T(8,128)}) %all-gather.11.cloned.1.call-update) | async-done | bytes 6291472 | tf_op jit(solution)/shard_map/all_gather | solution.py:72
  768.9 2.4 fusion
  771.4 1.6 fusion.21
  773.0 0.9 copy.33
  773.9 0.1 pad_maximum_fusion
  774.0 1.4 copy.29
  775.3 44.9 %all-gather.17.cloned.1.call-done = f32[4096,256]{1,0:T(8,128)} async-done(((f32[256,256]{1,0:T(8,128)}), f32[4096,256]{1,0:T(8,128)}) %all-gather.17.cloned.1.call-update) | async-done | bytes 4194320 | tf_op jit(solution)/shard_map/all_gather | solution.py:79
  820.3 2.6 reduce_sum.39
  822.9 1.0 bitcast_subtract_fusion
  823.9 91.6 %all-reduce.3.cloned.1.call-done = (f32[256,256]{0,1:T(8,128)}, f32[2,256,256]{2,1,0:T(8,128)}) async-done(((f32[256,256]{0,1:T(8,128)}, f32[2,256,256]{2,1,0:T(8,128)}), (f32[256,256]{0,1:T(8,128)}, f32[2,256,256]{2,1,0:T(8,128)})) %all-reduce.3.cloned.1.call-update) | async-done | bytes 786448 | tf_op jit(solution)/shard_map/psum | solution.py:77
  915.5 1.5 fusion.7
  917.1 0.8 copy.27
  917.9 49.3 %all-gather.15.cloned.1.call-done = f32[4096,256]{1,0:T(8,128)} async-done(((f32[256,256]{1,0:T(8,128)}), f32[4096,256]{1,0:T(8,128)}) %all-gather.15.cloned.1.call-update) | async-done | bytes 4194320 | tf_op jit(solution)/shard_map/all_gather | solution.py:79
  967.2 3.2 reduce_sum.38
  970.4 1.6 convolution_add_fusion.3
  972.0 0.4 fusion.3
  972.4 1.6 fusion.6
  974.1 0.7 copy-done.5
  974.8 0.4 convolution_add_fusion.5
  975.2 0.4 fusion.5
  975.6 42.9 %all-gather.13.cloned.1.call-done = f32[4096,256]{1,0:T(8,128)} async-done(((f32[256,256]{1,0:T(8,128)}), f32[4096,256]{1,0:T(8,128)}) %all-gather.13.cloned.1.call-update) | async-done | bytes 4194320 | tf_op jit(solution)/shard_map/all_gather | solution.py:79
  1018.5 3.2 reduce_sum.37
  1021.7 1.8 copy.23
  1023.5 1.6 fusion.4
  1025.1 0.6 fusion.2
  1025.7 0.1 pad_maximum_fusion.1
  1025.8 0.3 copy.28
  1026.1 0.6 copy-done.6
  1026.7 0.1 copy-done.7
  1026.7 1.6 maximum_maximum_fusion
  (24 shorter events, 0.2 us)
Async XLA Ops:
  7.2 403.6 %reduce-scatter.8.cloned.1.call-start = ((), (), s32[]{:S(2)}) async-start(), calls=%async_computation.6 | async-start | bytes 6684672 | tf_op jit(solution)/shard_map/reduce_scatter | solution.py:61
  27.6 1.3 copy-start.2
  27.7 526.5 %reduce-scatter.6.cloned.1.call-start = ((), (), s32[]{:S(2)}) async-start(), calls=%async_computation.5 | async-start | bytes 6684672 | tf_op jit(solution)/shard_map/reduce_scatter | solution.py:61
  56.6 564.1 %all-to-all-start = ((f32[16,384,768]{2,1,0:T(8,128)}), f32[16,384,768]{2,1,0:T(8,128)}, u32[]{:S(2)}, u32[]{:S(2)}) async-start(f32[16,384,768]{2,1,0:T(8,128)} %broadcast_multiply_fusion), calls=%async_computation.3 | async-start | bytes 37748736 | tf_op jit(solution)/shard_map/all_to_all | solution.py:44
  64.0 554.0 %all-gather.9.cloned.1.call-start = ((), (), s32[]{:S(2)}) async-start(), calls=%async_computation.7 | async-start | bytes 6684672 | tf_op jit(solution)/shard_map/all_gather | solution.py:72
  412.6 292.9 %reduce-scatter.4.cloned.1.call-start = ((), (), s32[]{:S(2)}) async-start(), calls=%async_computation.4 | async-start | bytes 6684672 | tf_op jit(solution)/shard_map/reduce_scatter | solution.py:61
  432.2 336.8 %all-gather.11.cloned.1.call-start = ((), (), s32[]{:S(2)}) async-start(), calls=%async_computation.8 | async-start | bytes 6684672 | tf_op jit(solution)/shard_map/all_gather | solution.py:72
  620.6 8.1 copy-start.1
  620.6 9.7 copy-start
  620.6 199.6 %all-gather.17.cloned.1.call-start = ((), (), s32[]{:S(2)}) async-start(), calls=%async_computation.11 | async-start | bytes 4456448 | tf_op jit(solution)/shard_map/all_gather | solution.py:79
  630.3 285.2 %all-reduce.3.cloned.1.call-start = ((), (), s32[]{:S(2)}) async-start(), calls=%async_computation.12 | async-start | bytes 1572864 | tf_op jit(solution)/shard_map/psum | solution.py:77
  634.2 333.1 %all-gather.15.cloned.1.call-start = ((), (), s32[]{:S(2)}) async-start(), calls=%async_computation.10 | async-start | bytes 4456448 | tf_op jit(solution)/shard_map/all_gather | solution.py:79
  635.8 137.2 %slice-start = ((f32[3,256,256]{2,1,0:T(8,128)}), f32[1,256,256]{2,1,0:T(8,128)S(1)}, s32[]{:S(2)}) async-start(f32[3,256,256]{2,1,0:T(8,128)} %param.8), calls=%async_computation.13 | async-start | bytes 524288 | tf_op jit(solution)/shard_map/slice | solution.py:90
  635.8 382.7 %all-gather.13.cloned.1.call-start = ((), (), s32[]{:S(2)}) async-start(), calls=%async_computation.9 | async-start | bytes 4456448 | tf_op jit(solution)/shard_map/all_gather | solution.py:79
  771.4 2.5 copy-start.3
  820.3 95.3 %copy-start.4 = (f32[768,768]{1,0:T(8,128)S(1)}, f32[768,768]{1,0:T(8,128)}, u32[]{:S(2)}) copy-start(f32[768,768]{1,0:T(8,128)} %param.7) | copy-start | bytes 7077892
  970.4 4.4 copy-start.8
  974.1 0.7 copy-start.5
  1025.7 1.0 copy-start.6
  1025.7 1.0 copy-start.7
Sparse Core Ops, SparseCore 0:
  27.8 382.9 reduce-scatter.7
  415.3 138.8 reduce-scatter.5
  557.0 60.9 all-gather.8
  621.8 83.6 reduce-scatter.3
  708.0 60.9 all-gather.10
  771.2 49.0 all-gather.16
  824.8 90.7 all-reduce.2
  917.7 49.5 all-gather.14
  969.4 49.0 all-gather.12
